TPU v7x, 32 devices: a whole 2x2x4 slice. The times are simulated.
32 devices in a mesh: seq: 4 (over y, x), grp: 8 (over z, core).
Axes of the slice: x: 2, y: 2, z: 4, core: 2. Of those that a mesh axis runs over, the one named last changes fastest.
Arguments:
- actions: int32 [16, 7], P('grp'), may hold values from 0 to 255
- lengths: int32 [16], P('grp'), may hold values from 512 to 1024
- embed: bfloat16 [256, 4096], replicated, may hold values from -6 to 6
- attn_gain: float32 [4096], replicated, may hold values from 0.1 to 1.9
- w_query: bfloat16 [4096, 4096], P('grp', 'seq'), may hold values from -0.09375 to 0.09375
- w_key: bfloat16 [4096, 4096], P('grp', 'seq'), may hold values from -0.140625 to 0.140625
- w_value: bfloat16 [4096, 4096], P('grp', 'seq'), may hold values from -0.09375 to 0.09375
- w_out: bfloat16 [4096, 4096], P('grp', 'seq'), may hold values from -0.09375 to 0.09375
- key_cache: bfloat16 [16, 1024, 4096], P('grp', 'seq'), may hold values from -136 to 136
- value_cache: bfloat16 [16, 1024, 4096], P('grp', 'seq'), may hold values from -6 to 6
- final_gain: float32 [4096], replicated, may hold values from 0.1 to 1.9
- head: bfloat16 [256, 4096], P('seq'), may hold values from -0.25 to 0.25
Outputs:
- logprob: float32 [16, 7, 256], P('grp', None, 'seq')
Inputs may be any that keep to these rules, and one draw needn't show every extreme that they name: Robot r's prompt occupies cache positions 0 to lengths[r] - 1.
All inputs are finite; a program needn't handle non-finite values.
Results may differ from a plain program's by a relative error of at most 0.008.
Values may be sent and summed in bfloat16 or wider, within the bound.
A program may use at most 64 MiB of HBM per device.

v0:
```python
import jax
import jax.numpy as jnp
from jax import lax
from jax.sharding import PartitionSpec as P

HEAD_DIM = 128


def merged(shard, axis, combine):
    everything = jax.tree.map(lambda part: lax.all_gather(part, axis), shard)
    initial = jax.tree.map(lambda part: part[0], everything)

    def step(k, so_far):
        return combine(so_far, jax.tree.map(lambda part: part[k], everything))

    return lax.fori_loop(1, lax.axis_size(axis), step, initial)


def rms_scale(values, gain):
    mean_square = jnp.mean(values * values, axis=-1, keepdims=True)
    return values * lax.rsqrt(mean_square + 1e-05) * gain


def rotate(values, places):
    half = values.shape[-1] // 2
    freq = 10000.0 ** (-(jnp.arange(half, dtype=jnp.float32) * 2.0 / values.shape[-1]))
    angle = places[..., None, None] * freq
    first = values[..., :half]
    second = values[..., half:]
    cosine = jnp.cos(angle)
    sine = jnp.sin(angle)
    return jnp.concatenate(
        [first * cosine - second * sine, second * cosine + first * sine], axis=-1
    )


def join_softmax(left, right):
    top = jnp.maximum(left[0], right[0])
    left_factor = jnp.exp(left[0] - top)
    right_factor = jnp.exp(right[0] - top)
    total = left[1] * left_factor + right[1] * right_factor
    acc = left[2] * left_factor[..., None] + right[2] * right_factor[..., None]
    return (top, total, acc)


def join_totals(left, right):
    top = jnp.maximum(left[0], right[0])
    return (top, left[1] * jnp.exp(left[0] - top) + right[1] * jnp.exp(right[0] - top))


def on_device(
    actions,
    lengths,
    embed,
    attn_gain,
    w_query,
    w_key,
    w_value,
    w_out,
    key_cache,
    value_cache,
    final_gain,
    head,
):
    seq_index = lax.axis_index("seq")
    seq_count = lax.axis_size("seq")
    robots, steps = actions.shape
    prompt_dev = key_cache.shape[1]
    width = key_cache.shape[2]
    col_block = w_query.shape[1]
    head_dim = HEAD_DIM
    heads = width // head_dim
    local_heads = col_block // head_dim
    scale = head_dim ** (-0.5)
    bins = jnp.arange(embed.shape[0], dtype=jnp.int32)
    onehot = (actions[:, :, None] == bins[None, None, :]).astype(jnp.bfloat16)
    inputs = jnp.einsum("rtb,bd->rtd", onehot, embed, preferred_element_type=jnp.float32)
    normed = rms_scale(inputs, attn_gain).astype(jnp.bfloat16)
    places = (lengths[:, None] + jnp.arange(steps, dtype=jnp.int32)[None, :]).astype(jnp.float32)
    prompt_places = seq_index * prompt_dev + jnp.arange(prompt_dev, dtype=jnp.int32)
    prompt_valid = prompt_places[None, :] < lengths[:, None]
    cache_keys = key_cache.reshape(robots, prompt_dev, heads, head_dim)
    cache_values = value_cache.reshape(robots, prompt_dev, heads, head_dim)
    empty = jnp.zeros((robots, 0, heads, head_dim), jnp.bfloat16)
    window_keys = empty
    window_values = empty
    rows = robots * steps
    block_norm = normed.reshape(rows, width)
    spread_rows = lax.all_to_all(block_norm, "grp", split_axis=1, concat_axis=0, tiled=True)
    terms = jnp.concatenate(
        [
            jnp.dot(spread_rows, w_query, preferred_element_type=jnp.float32),
            jnp.dot(spread_rows, w_key, preferred_element_type=jnp.float32),
            jnp.dot(spread_rows, w_value, preferred_element_type=jnp.float32),
        ],
        axis=1,
    )
    sums = lax.psum_scatter(terms, "grp", scatter_dimension=0, tiled=True)

    def heads_of(flat):
        return flat.reshape(robots, steps, local_heads, head_dim)

    query = (
        rotate(heads_of(sums[:, :col_block]), places).astype(jnp.bfloat16).reshape(rows, col_block)
    )
    key = (
        rotate(heads_of(sums[:, col_block : 2 * col_block]), places)
        .astype(jnp.bfloat16)
        .reshape(rows, col_block)
    )
    value = sums[:, 2 * col_block :].astype(jnp.bfloat16)
    query, key, value = (
        lax.all_gather(query, "seq", axis=1, tiled=True),
        lax.all_gather(key, "seq", axis=1, tiled=True),
        lax.all_gather(value, "seq", axis=1, tiled=True),
    )
    query = query.reshape(robots, steps, heads, head_dim)
    window_keys = jnp.concatenate(
        [window_keys, key.reshape(robots, steps, heads, head_dim)], axis=1
    )
    window_values = jnp.concatenate(
        [window_values, value.reshape(robots, steps, heads, head_dim)], axis=1
    )
    seen = 0 + steps
    window_index = jnp.arange(seen, dtype=jnp.int32)
    step_index = 0 + jnp.arange(steps, dtype=jnp.int32)
    window_valid = (window_index[None, :] <= step_index[:, None]) & (
        window_index % seq_count == seq_index
    )[None, :]
    prompt_mask = prompt_valid[:, None, None, :]
    window_mask = window_valid[None, :, None, :]
    prompt_scores = (
        jnp.einsum("rthd,rphd->rthp", query, cache_keys, preferred_element_type=jnp.float32) * scale
    )
    window_scores = (
        jnp.einsum("rthd,rjhd->rthj", query, window_keys, preferred_element_type=jnp.float32)
        * scale
    )
    prompt_scores = jnp.where(prompt_mask, prompt_scores, -1e30)
    window_scores = jnp.where(window_mask, window_scores, -1e30)
    local_max = jnp.maximum(jnp.max(prompt_scores, axis=-1), jnp.max(window_scores, axis=-1))
    prompt_e = jnp.where(prompt_mask, jnp.exp(prompt_scores - local_max[..., None]), 0.0)
    window_e = jnp.where(window_mask, jnp.exp(window_scores - local_max[..., None]), 0.0)
    total = jnp.sum(prompt_e, axis=-1) + jnp.sum(window_e, axis=-1)
    acc = jnp.einsum(
        "rthp,rphd->rthd",
        prompt_e.astype(jnp.bfloat16),
        cache_values,
        preferred_element_type=jnp.float32,
    )
    acc = acc + jnp.einsum(
        "rthj,rjhd->rthd",
        window_e.astype(jnp.bfloat16),
        window_values,
        preferred_element_type=jnp.float32,
    )
    total, acc = (total, acc)
    top, total, acc = merged((local_max, total, acc), "seq", join_softmax)
    attended = (acc / total[..., None]).astype(jnp.bfloat16).reshape(rows, width)
    spread_attended = lax.all_to_all(attended, "grp", split_axis=1, concat_axis=0, tiled=True)
    out_terms = jnp.dot(spread_attended, w_out, preferred_element_type=jnp.float32)
    out_part = lax.psum_scatter(
        out_terms.astype(jnp.bfloat16), "grp", scatter_dimension=0, tiled=True
    ).astype(jnp.float32)
    branch = lax.all_gather(out_part, "seq", axis=1, tiled=True)
    residual = inputs.reshape(rows, width) + branch
    final = rms_scale(residual, final_gain).astype(jnp.bfloat16)
    logits = lax.dot_general(
        final, head, (((1,), (1,)), ((), ())), preferred_element_type=jnp.float32
    )
    row_max = jnp.max(logits, axis=-1)
    local_total = jnp.sum(jnp.exp(logits - row_max[:, None]), axis=-1)
    top_logit, exp_total = merged((row_max, local_total), "seq", join_totals)
    logprob = logits - top_logit[:, None] - jnp.log(exp_total)[:, None]
    result = logprob.reshape(robots, steps, logits.shape[1])
    return result


def solution(mesh):
    placed = (
        P("grp", None),
        P("grp"),
        P(),
        P(),
        P("grp", "seq"),
        P("grp", "seq"),
        P("grp", "seq"),
        P("grp", "seq"),
        P("grp", "seq", None),
        P("grp", "seq", None),
        P(),
        P("seq", None),
    )
    return jax.shard_map(
        on_device, mesh=mesh, in_specs=placed, out_specs=P("grp", None, "seq"), check_vma=False
    )
```

profile of v0, /device:TPU:0, one launch (start us, length us, event | category | flops | bytes accessed | tf_op | source)
XLA Modules:
  0.0 219.2 jit_solution(14743397479627229523)
XLA Ops:
  6.5 1.6 copy-done
  8.1 1.2 multiply_reduce_fusion.1
  9.3 0.8 multiply_convert_fusion.1
  10.2 0.8 all_to_all.28
  10.9 1.6 copy.61
  12.5 6.3 %all-to-all-start = ((bf16[14,8,512]{2,0,1:T(8,128)(2,1)}), bf16[14,8,512]{2,0,1:T(8,128)(2,1)S(1)}, u32[]{:S(2)}, u32[]{:S(2)}) async-start(bf16[14,8,512]{2,0,1:T(8,128)(2,1)} %copy.61), calls=%async_computation | async-start | bytes 262144 | tf_op jit(solution)/shard_map/all_to_all | solution.py:89
  18.9 0.7 add_convert_fusion.2
  19.7 6.0 %all-to-all-done = bf16[14,8,512]{2,0,1:T(8,128)(2,1)S(1)} async-done(((bf16[14,8,512]{2,0,1:T(8,128)(2,1)}), bf16[14,8,512]{2,0,1:T(8,128)(2,1)S(1)}, u32[]{:S(2)}, u32[]{:S(2)}) %all-to-all-start) | async-done | bytes 114720 | tf_op jit(solution)/shard_map/all_to_all | solution.py:89
  25.6 0.6 copy-done.3
  26.3 0.9 all_to_all.31
  27.2 0.3 fusion.54
  27.6 1.5 fusion.55
  29.1 1.5 fusion.56
  30.6 1.2 pad_maximum_fusion
  31.9 0.7 fusion.51
  33.3 58.2 %all-reduce.8.cloned.1.call-done = f32[112,3072]{1,0:T(8,128)} async-done(((f32[112,3072]{1,0:T(8,128)}), f32[112,3072]{1,0:T(8,128)}) %all-reduce.8.cloned.1.call-update) | async-done | bytes 1376272
  91.5 1.0 fusion.50
  92.8 8.4 %all_gather.38 = bf16[14,4096]{1,0:T(8,128)(2,1)S(1)} all-gather(bf16[14,1024]{1,0:T(8,128)(2,1)S(1)} %bitcast.154), channel_id=1, replica_groups=mesh['seq'=4,'grp'=8] {'seq'}, dimensions={1}, use_global_device_ids=true | all-gather | bytes 143360 | tf_op jit(solution)/shard_map/all_gather | solution.py:113
  101.3 8.4 %all_gather.39 = bf16[14,4096]{1,0:T(8,128)(2,1)S(1)} all-gather(bf16[14,1024]{1,0:T(8,128)(2,1)S(1)} %bitcast.155), channel_id=1, replica_groups=mesh['seq'=4,'grp'=8] {'seq'}, dimensions={1}, use_global_device_ids=true | all-gather | bytes 143360 | tf_op jit(solution)/shard_map/all_gather | solution.py:114
  110.4 3.5 %fusion.52 = (f32[2,7,32]{1,2,0:T(8,128)S(1)}, f32[2,7,32,256]{3,1,2,0:T(8,128)S(1)}) fusion(bf16[2,7,32,128]{3,2,1,0:T(8,128)(2,1)S(1)} %bitcast.135, pred[2,256]{1,0:T(4,128)(4,1)S(1)} %broadcast_compare_fusion, bf16[2,256,4096]{2,1,0:T(8,128)(2,1)} %param.24), kind=kOutput, calls=%fused_computation.82 | convolution fusion | flops 29703744 | bytes 4770048 | tf_op jit(solution)/shard_map/rthd,rphd->rthp/dot_general | solution.py:133
  114.0 0.7 copy.68
  115.0 1.0 dynamic-slice.16
  116.0 7.9 %all_gather.42 = bf16[14,4096]{1,0:T(8,128)(2,1)S(1)} all-gather(bf16[14,1024]{1,0:T(8,128)(2,1)S(1)} %dynamic-slice.16), channel_id=1, replica_groups=mesh['seq'=4,'grp'=8] {'seq'}, dimensions={1}, use_global_device_ids=true | all-gather | bytes 143360 | tf_op jit(solution)/shard_map/all_gather | solution.py:115
  123.9 0.3 fusion.30
  124.4 2.9 %fusion.26 = f32[2,7,32,128]{3,1,2,0:T(8,128)S(1)} fusion(f32[2,7,32,128]{3,1,2,0:T(8,128)S(1)} %convolution_bitcast_fusion, f32[2,7,32,256]{3,1,2,0:T(8,128)S(1)} %get-tuple-element.384, f32[2,7,32]{1,2,0:T(8,128)S(1)} %max.37, pred[2,256]{1,0:T(4,128)(4,1)S(1)} %broadcast_compare_fusion, bf16[2,256,4096]{2,1,0:T(8,128)(2,1)} %param.25), kind=kOutput, calls=%fused_computation.28 | convolution fusion | flops 29761536 | bytes 5114112 | tf_op jit(solution)/shard_map/rthp,rphd->rthd/dot_general | solution.py:145
  127.3 11.7 %all-gather.2 = f32[8,7,32,128]{3,2,1,0:T(8,128)S(1)} all-gather(f32[2,7,32,128]{3,2,1,0:T(8,128)S(1)} %copy.75), channel_id=4, replica_groups=mesh['seq'=4,'grp'=8] {'seq'}, dimensions={0}, use_global_device_ids=true | all-gather | bytes 1146880 | tf_op jit(solution)/shard_map/all_gather | solution.py:10
  139.0 0.7 copy.79
  139.7 1.4 add.190
  141.1 0.8 copy.71
  141.9 7.2 %all-gather.1 = f32[8,7,32]{2,1,0:T(8,128)S(1)} all-gather(f32[2,7,32]{2,1,0:T(8,128)S(1)} %copy.71), channel_id=3, replica_groups=mesh['seq'=4,'grp'=8] {'seq'}, dimensions={0}, use_global_device_ids=true | all-gather | bytes 8960 | tf_op jit(solution)/shard_map/all_gather | solution.py:10
  149.1 8.1 %all-gather = f32[8,7,32]{2,1,0:T(8,128)S(1)} all-gather(f32[2,7,32]{2,1,0:T(8,128)} %copy.68), channel_id=2, replica_groups=mesh['seq'=4,'grp'=8] {'seq'}, dimensions={0}, use_global_device_ids=true | all-gather | bytes 8960 | tf_op jit(solution)/shard_map/all_gather | solution.py:10
  157.3 0.6 copy-done.4
  157.9 2.9 %while.36 = (s32[]{:T(128)}, f32[2,7,32]{2,1,0:T(8,128)S(1)}, f32[2,7,32]{2,1,0:T(8,128)S(1)}, f32[2,7,32,128]{3,2,1,0:T(8,128)S(1)}, f32[4,2,7,32]{3,2,1,0:T(8,...) while((s32[]{:T(128)}, f32[2,7,32]{2,1,0:T(8,128)S(1)}, ...), condition=%wide.region_7.8_spmd, body=%wide.region_6.7_spmd.sunk | while | flops 174725 | bytes 706199 | solution.py:16
  157.9 0.7 fusion.72
  158.6 0.2 fusion.73
  158.8 0.7 fusion.72
  159.8 0.7 fusion.72
  160.5 0.2 fusion.73
  161.1 9.3 %all_to_all.38 = bf16[14,8,512]{2,0,1:T(8,128)(2,1)S(1)} all-to-all(bf16[14,8,512]{2,0,1:T(8,128)(2,1)S(1)} %copy.76), channel_id=1, replica_groups=mesh['seq'=4,'grp'=8] {'grp'}, dimensions={1} | all-to-all | bytes 229376 | tf_op jit(solution)/shard_map/all_to_all | solution.py:160
  170.4 1.5 convolution_convert_fusion
  171.9 16.7 %fusion = bf16[16,1024]{1,0:T(8,128)(2,1)S(1)} fusion(bf16[112,1024]{1,0:T(8,128)(2,1)S(1)} %convolution_convert_fusion), kind=kCustom, calls=%all-reduce-scatter | all-reduce-scatter fusion | flops 131073 | bytes 262656
  188.7 1.3 collective-permute-start
  190.7 1.3 dynamic-slice
  192.9 8.2 %all_gather.45 = f32[14,4096]{1,0:T(8,128)S(1)} all-gather(f32[14,1024]{1,0:T(8,128)S(1)} %dynamic-slice_convert_fusion.1), channel_id=1, replica_groups=mesh['seq'=4,'grp'=8] {'seq'}, dimensions={1}, use_global_device_ids=true | all-gather | bytes 286720 | tf_op jit(solution)/shard_map/all_gather | solution.py:165
  201.3 0.4 fusion.53
  201.9 0.2 dynamic-update-slice
  202.3 9.1 %all-reduce.5 = (f32[56]{0:T(128)S(1)}, f32[56]{0:T(128)S(1)}) all-reduce(f32[56]{0:T(128)S(1)} %dynamic-update-slice, f32[56]{0:T(128)S(1)} %dynamic-update-slice.1), channel_id=5, replica_groups=mesh['seq'=4,'grp'=8] {'seq'}, use_global_device_ids=true, to_apply=%add | all-reduce | flops 112 | bytes 896
  211.8 0.6 copy.77
  (76 shorter events, 3.8 us)
Async XLA Ops:
  6.5 1.6 copy-start
  6.5 20.7 %copy-start.1 = (bf16[512,1024]{1,0:T(8,128)(2,1)S(1)}, bf16[512,1024]{1,0:T(8,128)(2,1)}, u32[]{:S(2)}) copy-start(bf16[512,1024]{1,0:T(8,128)(2,1)} %param.20) | copy-start | bytes 3145732
  12.5 13.1 %all-to-all-start = ((bf16[14,8,512]{2,0,1:T(8,128)(2,1)}), bf16[14,8,512]{2,0,1:T(8,128)(2,1)S(1)}, u32[]{:S(2)}, u32[]{:S(2)}) async-start(bf16[14,8,512]{2,0,1:T(8,128)(2,1)} %copy.61), calls=%async_computation | async-start | bytes 262144 | tf_op jit(solution)/shard_map/all_to_all | solution.py:89
  18.8 72.7 %all-reduce.8.cloned.1.call-start = ((), (), s32[]{:S(2)}) async-start(), calls=%async_computation.2 | async-start | bytes 2752512
  25.6 0.6 copy-start.3
  27.2 4.7 %copy-start.6 = (u32[32]{0:T(128)S(1)}, u32[32]{0:T(128)}, u32[]{:S(2)}) copy-start(u32[32]{0:T(128)} %constant.137) | copy-start | bytes 388
  27.2 5.9 %copy-start.7 = (s32[2]{0:T(128)S(1)}, s32[2]{0:T(128)}, u32[]{:S(2)}) copy-start(s32[2]{0:T(128)} %param.17) | copy-start | bytes 28
  157.3 0.6 copy-start.4
  160.8 40.5 %copy-start.2 = (bf16[64,4096]{1,0:T(8,128)(2,1)S(1)}, bf16[64,4096]{1,0:T(8,128)(2,1)}, u32[]{:S(2)}) copy-start(bf16[64,4096]{1,0:T(8,128)(2,1)} %param.27) | copy-start | bytes 1572868
  160.8 40.5 %copy-start.5 = (f32[4096]{0:T(1024)S(1)}, f32[4096]{0:T(1024)}, u32[]{:S(2)}) copy-start(f32[4096]{0:T(1024)} %param.26) | copy-start | bytes 49156
  188.7 4.0 %collective-permute-start = (bf16[14,1024]{1,0:T(8,128)(2,1)S(1)}, bf16[14,1024]{1,0:T(8,128)(2,1)S(1)}, u32[]{:S(2)}, u32[]{:S(2)}) collective-permute-start(bf16[14,1024]{1,0:T(8,128)(2,1)S(1)} %slice.61), channel_id=1, source_target_pairs={{0,1},{1,2},{2,3},{3,4},{4,5},{5,6},{6,7},{8,9},{9,10},{10,11},{11... | collective-permute-start | bytes 86024
Sparse Core Ops, SparseCore 0:
  32.0 59.4 all-reduce.7
where the time goes:
time: 220 us; the launch traced here: 219 us
  blocking collectives  94.9 us (43%)
  waiting for transfers between devices  64.2 us (29%)
  between operations  15.8 us (7%)
  local copies, waits for them, and re-layouts  14.7 us (7%)
  matrix products  13.3 us (6%)
  other arithmetic  8.59 us (4%)
  starting transfers between devices  7.65 us (3%)
    unnamed x3, waiting for transfers between devices  58.2 us
    all_gather x3, blocking collectives, merged(): everything = jax.tree.map(lambda part: lax.all_gather(part, axis), shard)  27 us
    unnamed x2, blocking collectives  25.8 us
    all_to_all x1, blocking collectives, on_device(): lax.all_to_all(attended, 'grp', split_axis=1, concat_axis=0, tiled=True)  9.25 us
    all_gather x1, blocking collectives, on_device(): lax.all_gather(key, 'seq', axis=1, tiled=True)  8.42 us
    all_gather x1, blocking collectives, on_device(): lax.all_gather(query, 'seq', axis=1, tiled=True)  8.42 us
    all_gather x1, blocking collectives, on_device(): branch = lax.all_gather(out_part, 'seq', axis=1, tiled=True)  8.15 us
    all_gather x1, blocking collectives, on_device(): lax.all_gather(value, 'seq', axis=1, tiled=True)  7.86 us
  transfers between devices with their start and end apart: 3, of which 2 were waited for; matrix products, arithmetic and copies ran while one was open for 1% of the time, Pallas kernels for 0%

commit v1 on v0

v1 whole, which is shorter than its diff:
```python
import functools

import jax
import jax.numpy as jnp
from jax import lax
from jax.experimental import pallas as pl
from jax.experimental.pallas import tpu as pltpu
from jax.sharding import PartitionSpec as P

HEAD_DIM = 128
PAD = 8
MESH = pl.DeviceIdType.MESH
NEG = -1e30


def dot(a, b):
    return lax.dot_general(a, b, (((1,), (0,)), ((), ())), preferred_element_type=jnp.float32)


def dot_t(a, b):
    return lax.dot_general(a, b, (((1,), (1,)), ((), ())), preferred_element_type=jnp.float32)


def kernel(
    S,
    G,
    acts,
    lens,
    cos_ref,
    sin_ref,
    gain_ref,
    fgain_ref,
    embed_h,
    wq_h,
    wk_h,
    wv_h,
    wo_h,
    kc_h,
    vc_h,
    head_h,
    out_ref,
    embed,
    w3,
    wo,
    kc,
    vc,
    head,
    acts_all,
    part,
    got,
    kv,
    qall,
    acc_out,
    acc_in,
    st_out,
    st_in,
    att,
    attall,
    obuf,
    ogot,
    resall,
    fin,
    lse,
    load_sem,
    a_send,
    a_recv,
    b_send,
    b_recv,
    c_send,
    c_recv,
    d_send,
    d_recv,
    e_send,
    e_recv,
    f_send,
    f_recv,
    g_send,
    g_recv,
    h_send,
    h_recv,
):
    s = lax.axis_index("seq")
    g = lax.axis_index("grp")
    RW = acts.shape[0]
    robots = RW // PAD
    bins, width = embed.shape
    CB = wo.shape[1]
    RB = wo.shape[0]
    ratio = CB // RB
    LH = CB // HEAD_DIM
    pos = kc.shape[1]
    scale = HEAD_DIM ** (-0.5)

    loads = []
    for i, (src, dst) in enumerate(
        [
            (embed_h, embed),
            (wq_h, w3.at[0]),
            (wk_h, w3.at[1]),
            (wv_h, w3.at[2]),
            (kc_h, kc),
            (vc_h, vc),
            (wo_h, wo),
            (head_h, head),
        ]
    ):
        copy = pltpu.make_async_copy(src, dst, load_sem.at[i])
        copy.start()
        loads.append(copy)

    barrier = pltpu.get_barrier_semaphore()
    total_devices = S * G
    flat = s * G + g

    def greet(d, carry):
        other = lax.rem(flat + d, total_devices)
        pl.semaphore_signal(
            barrier,
            inc=1,
            device_id={"seq": other // G, "grp": lax.rem(other, G)},
            device_id_type=MESH,
        )
        return carry

    lax.fori_loop(1, total_devices, greet, 0)
    pl.semaphore_wait(barrier, total_devices - 1)

    pending = []

    def push(axis, n, me, src_of, dst, send, recv):
        copies = []
        for k in range(1, n):
            peer = lax.rem(me + k, n)
            copy = pltpu.make_async_remote_copy(
                src_ref=src_of(peer),
                dst_ref=dst,
                send_sem=send.at[k],
                recv_sem=recv.at[k],
                device_id={axis: peer},
                device_id_type=MESH,
            )
            copy.start()
            copies.append(copy)
            pending.append(copy)
        return copies

    acts_all[g] = acts[...]
    ca = push("grp", G, g, lambda p: acts, acts_all.at[g], a_send, a_recv)

    loads[0].wait()
    squares = jnp.zeros((bins, 128), jnp.float32)
    for c in range(width // 128):
        x = embed[:, c * 128 : (c + 1) * 128].astype(jnp.float32)
        squares = squares + x * x
    inv = lax.rsqrt(jnp.sum(squares, axis=-1, keepdims=True) * (1.0 / width) + 1e-05)
    block = pl.ds(pl.multiple_of(g * RB, RB), RB)
    table = (embed[:, block].astype(jnp.float32) * inv * gain_ref[:, block]).astype(jnp.bfloat16)
    for c in ca:
        c.wait_recv()
    lane_bin = lax.broadcasted_iota(jnp.int32, (G * RW, bins), 1)
    picked = acts_all[...].reshape(G * RW, 128)[:, :1]
    onehot = jnp.where(lane_bin == picked, 1.0, 0.0).astype(jnp.bfloat16)
    rows = dot(onehot, table).astype(jnp.bfloat16)
    cb = []
    for i in range(3):
        loads[1 + i].wait()
        part[i] = dot(rows, w3[i]).astype(jnp.bfloat16).reshape(G, RW, CB)
        cb.append(
            push(
                "grp", G, g, lambda p, i=i: part.at[i, p], got.at[i, g], b_send.at[i], b_recv.at[i]
            )
        )
    cols = pl.ds(pl.multiple_of(s * CB, CB), CB)
    own_hot = jnp.where(
        lax.broadcasted_iota(jnp.int32, (RW, bins), 1) == acts[:, :1], 1.0, 0.0
    ).astype(jnp.bfloat16)
    inputs = dot(own_hot, embed[:, cols])

    def summed(i):
        for c in cb[i]:
            c.wait_recv()
        total = part[i, g].astype(jnp.float32)
        for k in range(1, G):
            total = total + got[i, lax.rem(g + (G - k), G)].astype(jnp.float32)
        return total

    def rotated(x):
        parts = []
        for j in range(LH):
            y = x[:, j * HEAD_DIM : (j + 1) * HEAD_DIM]
            parts.append(y * cos_ref[...] + pltpu.roll(y, HEAD_DIM // 2, 1) * sin_ref[...])
        return jnp.concatenate(parts, axis=1).astype(jnp.bfloat16)

    qall[s] = rotated(summed(0))
    cc = push("seq", S, s, lambda p: qall.at[s], qall.at[s], c_send, c_recv)

    lane = lax.broadcasted_iota(jnp.int32, (PAD, 128), 1)
    place = lax.broadcasted_iota(jnp.int32, (PAD, pos), 1) + s * pos
    valid = [place < lens[r * PAD : (r + 1) * PAD, :1] for r in range(robots)]
    loads[4].wait()
    loads[5].wait()

    def attend(owner):
        q = qall[owner].astype(jnp.float32)
        for r in range(robots):
            low = r * PAD
            tops = jnp.zeros((PAD, 128), jnp.float32)
            totals = jnp.zeros((PAD, 128), jnp.float32)
            for j in range(LH):
                lanes = pl.ds(pl.multiple_of(owner * CB + j * HEAD_DIM, HEAD_DIM), HEAD_DIM)
                qh = q[low : low + PAD, j * HEAD_DIM : (j + 1) * HEAD_DIM].astype(jnp.bfloat16)
                score = jnp.where(valid[r], dot_t(qh, kc[r, :, lanes]) * scale, NEG)
                top = jnp.max(score, axis=-1, keepdims=True)
                e = jnp.where(valid[r], jnp.exp(score - top), 0.0)
                tops = jnp.where(lane == j, top, tops)
                totals = jnp.where(lane == j, jnp.sum(e, axis=-1, keepdims=True), totals)
                acc_out[owner, low : low + PAD, j * HEAD_DIM : (j + 1) * HEAD_DIM] = dot(
                    e.astype(jnp.bfloat16), vc[r, :, lanes]
                )
            st_out[owner, 0, low : low + PAD, :] = tops
            st_out[owner, 1, low : low + PAD, :] = totals

    attend(s)
    cd = []
    for k in range(1, S):
        cc[k - 1].wait_recv()
        owner = lax.rem(s + (S - k), S)
        attend(owner)
        for i, (src, dst) in enumerate([(acc_out, acc_in), (st_out, st_in)]):
            copy = pltpu.make_async_remote_copy(
                src_ref=src.at[owner],
                dst_ref=dst.at[s],
                send_sem=d_send.at[i, k],
                recv_sem=d_recv.at[i, k],
                device_id={"seq": owner},
                device_id_type=MESH,
            )
            copy.start()
            cd.append(copy)
            pending.append(copy)

    kv[0] = rotated(summed(1))
    kv[1] = summed(2).astype(jnp.bfloat16)
    qi = lax.broadcasted_iota(jnp.int32, (RW, RW), 0)
    kj = lax.broadcasted_iota(jnp.int32, (RW, RW), 1)
    causal = (qi // PAD == kj // PAD) & (kj <= qi)
    wide = lax.broadcasted_iota(jnp.int32, (RW, 128), 1)
    w_top = jnp.zeros((RW, 128), jnp.float32)
    w_total = jnp.zeros((RW, 128), jnp.float32)
    w_acc = []
    for j in range(LH):
        hl = slice(j * HEAD_DIM, (j + 1) * HEAD_DIM)
        score = jnp.where(causal, dot_t(qall[s, :, hl], kv[0, :, hl]) * scale, NEG)
        top = jnp.max(score, axis=-1, keepdims=True)
        e = jnp.where(causal, jnp.exp(score - top), 0.0)
        w_top = jnp.where(wide == j, top, w_top)
        w_total = jnp.where(wide == j, jnp.sum(e, axis=-1, keepdims=True), w_total)
        w_acc.append(dot(e.astype(jnp.bfloat16), kv[1, :, hl]))

    for c in cd:
        c.wait_recv()
    sources = [lax.rem(s + k, S) for k in range(1, S)]
    top = jnp.maximum(w_top, st_out[s, 0])
    for o in sources:
        top = jnp.maximum(top, st_in[o, 0])
    w_f = jnp.exp(w_top - top)
    own_f = jnp.exp(st_out[s, 0] - top)
    fs = [jnp.exp(st_in[o, 0] - top) for o in sources]
    total = w_total * w_f + st_out[s, 1] * own_f
    for o, f in zip(sources, fs):
        total = total + st_in[o, 1] * f
    for j in range(LH):
        hl = slice(j * HEAD_DIM, (j + 1) * HEAD_DIM)
        acc = w_acc[j] * w_f[:, j : j + 1] + acc_out[s, :, hl] * own_f[:, j : j + 1]
        for o, f in zip(sources, fs):
            acc = acc + acc_in[o, :, hl] * f[:, j : j + 1]
        at = j * HEAD_DIM
        att[at // RB, :, at % RB : at % RB + HEAD_DIM] = (acc / total[:, j : j + 1]).astype(
            jnp.bfloat16
        )

    home = g // ratio
    for i in range(ratio):
        for k in range(S):
            s2 = lax.rem(s + k, S)
            g2 = s * ratio + i
            if k == 0:

                @pl.when(g2 == g)
                def _():
                    attall[g] = att[i]

            def send(i=i, k=k, s2=s2, g2=g2):
                return pltpu.make_async_remote_copy(
                    src_ref=att.at[i],
                    dst_ref=attall.at[g],
                    send_sem=e_send.at[i, k],
                    recv_sem=e_recv.at[g],
                    device_id={"seq": s2, "grp": g2},
                    device_id_type=MESH,
                )

            if k == 0:

                @pl.when(g2 != g)
                def _():
                    send().start()
            else:
                send().start()

    def arrival(q):
        return pltpu.make_async_remote_copy(
            src_ref=att.at[0],
            dst_ref=attall.at[q],
            send_sem=e_send.at[0, 0],
            recv_sem=e_recv.at[q],
            device_id={"seq": s, "grp": g},
            device_id_type=MESH,
        )

    for q in range(G):

        @pl.when(jnp.logical_or(home != s, g != q))
        def _():
            arrival(q).wait_recv()

    loads[6].wait()
    loads[7].wait()
    obuf[...] = (
        dot(attall[...].reshape(G * RW, RB), wo[...]).astype(jnp.bfloat16).reshape(G, RW, CB)
    )
    cf = push("grp", G, g, lambda p: obuf.at[p], ogot.at[g], f_send, f_recv)
    for c in cf:
        c.wait_recv()
    branch = obuf[g].astype(jnp.float32)
    for k in range(1, G):
        branch = branch + ogot[lax.rem(g + k, G)].astype(jnp.float32)
    resall[s] = inputs + branch
    cg = push("seq", S, s, lambda p: resall.at[s], resall.at[s], g_send, g_recv)
    for c in cg:
        c.wait_recv()
    squares = jnp.zeros((RW, CB), jnp.float32)
    for o in range(S):
        squares = squares + resall[o] * resall[o]
    inv = lax.rsqrt(jnp.sum(squares, axis=-1, keepdims=True) * (1.0 / width) + 1e-05)
    for o in range(S):
        hl = slice(o * CB, (o + 1) * CB)
        fin[:, hl] = (resall[o] * inv * fgain_ref[:, hl]).astype(jnp.bfloat16)
    logits = dot_t(fin[...], head[...])
    row_max = jnp.max(logits, axis=-1, keepdims=True)
    row_sum = jnp.sum(jnp.exp(logits - row_max), axis=-1, keepdims=True)
    lse[s, 0] = jnp.broadcast_to(row_max, (RW, 128))
    lse[s, 1] = jnp.broadcast_to(row_sum, (RW, 128))
    ch = push("seq", S, s, lambda p: lse.at[s], lse.at[s], h_send, h_recv)
    for c in ch:
        c.wait_recv()
    top = lse[0, 0]
    for o in range(1, S):
        top = jnp.maximum(top, lse[o, 0])
    total = lse[0, 1] * jnp.exp(lse[0, 0] - top)
    for o in range(1, S):
        total = total + lse[o, 1] * jnp.exp(lse[o, 0] - top)
    out_ref[...] = logits - top[:, :1] - jnp.log(total)[:, :1]

    for c in pending:
        c.wait_send()
    for i in range(ratio):
        for k in range(S):

            def sent(i=i, k=k):
                pltpu.make_async_remote_copy(
                    src_ref=att.at[i],
                    dst_ref=attall.at[g],
                    send_sem=e_send.at[i, k],
                    recv_sem=e_recv.at[g],
                    device_id={"seq": s, "grp": g},
                    device_id_type=MESH,
                ).wait_send()

            if k == 0:

                @pl.when(s * ratio + i != g)
                def _():
                    sent()
            else:
                sent()


def on_device(
    S,
    G,
    actions,
    lengths,
    embed,
    attn_gain,
    w_query,
    w_key,
    w_value,
    w_out,
    key_cache,
    value_cache,
    final_gain,
    head,
):
    robots, steps = actions.shape
    RW = robots * PAD
    bins, width = embed.shape
    RB, CB = w_out.shape
    ratio = CB // RB
    acts = jnp.pad(actions, ((0, 0), (0, PAD - steps))).reshape(RW, 1)
    acts = jnp.broadcast_to(acts, (RW, 128))
    lens = jnp.broadcast_to(jnp.repeat(lengths, PAD)[:, None], (RW, 128))
    half = HEAD_DIM // 2
    freq = 10000.0 ** (-(jnp.arange(half, dtype=jnp.float32) * 2.0 / HEAD_DIM))
    places = (lengths[:, None] + jnp.arange(PAD, dtype=jnp.int32)[None, :]).astype(jnp.float32)
    angle = places.reshape(RW, 1) * freq
    cosine = jnp.cos(angle)
    sine = jnp.sin(angle)
    cos2 = jnp.concatenate([cosine, cosine], axis=1)
    sin2 = jnp.concatenate([-sine, sine], axis=1)
    vmem = pl.BlockSpec(memory_space=pltpu.VMEM)
    hbm = pl.BlockSpec(memory_space=pl.ANY)
    bf, f32 = jnp.bfloat16, jnp.float32
    bins_dev = head.shape[0]
    V = pltpu.VMEM
    D = pltpu.SemaphoreType.DMA
    out = pl.pallas_call(
        functools.partial(kernel, S, G),
        out_shape=jax.ShapeDtypeStruct((RW, bins_dev), f32),
        in_specs=[vmem] * 6 + [hbm] * 8,
        out_specs=vmem,
        scratch_shapes=[
            V((bins, width), bf),
            V((3, RB, CB), bf),
            V((RB, CB), bf),
            V(key_cache.shape, bf),
            V(value_cache.shape, bf),
            V(head.shape, bf),
            V((G, RW, 128), jnp.int32),
            V((3, G, RW, CB), bf),
            V((3, G, RW, CB), bf),
            V((2, RW, CB), bf),
            V((S, RW, CB), bf),
            V((S, RW, CB), f32),
            V((S, RW, CB), f32),
            V((S, 2, RW, 128), f32),
            V((S, 2, RW, 128), f32),
            V((ratio, RW, RB), bf),
            V((G, RW, RB), bf),
            V((G, RW, CB), bf),
            V((G, RW, CB), bf),
            V((S, RW, CB), f32),
            V((RW, width), bf),
            V((S, 2, RW, 128), f32),
            D((8,)),
            D((G,)),
            D((G,)),
            D((3, G)),
            D((3, G)),
            D((S,)),
            D((S,)),
            D((2, S)),
            D((2, S)),
            D((ratio, S)),
            D((G,)),
            D((G,)),
            D((G,)),
            D((S,)),
            D((S,)),
            D((S,)),
            D((S,)),
        ],
        compiler_params=pltpu.CompilerParams(
            collective_id=0, has_side_effects=True, vmem_limit_bytes=48 * 2**20
        ),
    )(
        acts,
        lens,
        cos2,
        sin2,
        attn_gain.reshape(1, width),
        final_gain.reshape(1, width),
        embed,
        w_query,
        w_key,
        w_value,
        w_out,
        key_cache,
        value_cache,
        head,
    )
    return out.reshape(robots, PAD, bins_dev)[:, :steps]


def solution(mesh):
    placed = (
        P("grp", None),
        P("grp"),
        P(),
        P(),
        P("grp", "seq"),
        P("grp", "seq"),
        P("grp", "seq"),
        P("grp", "seq"),
        P("grp", "seq", None),
        P("grp", "seq", None),
        P(),
        P("seq", None),
    )
    return jax.shard_map(
        functools.partial(on_device, mesh.shape["seq"], mesh.shape["grp"]),
        mesh=mesh,
        in_specs=placed,
        out_specs=P("grp", None, "seq"),
        check_vma=False,
    )
```

time: 220 us -> 76 us (0.35)
  blocking collectives: 94.9 us -> 0 us
  Pallas kernels: 0 us -> 65.5 us
  waiting for transfers between devices: 64.2 us -> 0 us
  between operations: 15.8 us -> 0.03 us
  matrix products: 13.3 us -> 0 us
  other arithmetic: 8.59 us -> 0.22 us
  starting transfers between devices: 7.65 us -> 0 us
  local copies, waits for them, and re-layouts: 14.7 us -> 9.78 us
    pallas_call x0 -> x1, Pallas kernels: none -> 65.5 us  [on_device(): pl.pallas_call(functools.partial(kernel, S, G), out_shape=jax.ShapeDtypeS...]
    all_gather x7 -> x0, blocking collectives: 59.8 us -> none  [the longest x3 27 us: merged(): everything = jax.tree.map(lambda part: lax.all_gather(part, axis), shard)]
    unnamed x3 -> x0, waiting for transfers between devices: 58.2 us -> none
    unnamed x2 -> x0, blocking collectives: 25.8 us -> none
    dot_general x10 -> x0, matrix products: 13.3 us -> none  [the longest x1 3.46 us: on_device(): jnp.einsum('rthd,rphd->rthp', query, cache_keys, preferred_element_type=j...]
    all_to_all x1 -> x0, blocking collectives: 9.25 us -> none  [on_device(): lax.all_to_all(attended, 'grp', split_axis=1, concat_axis=0, tiled=True)]
    all_to_all x1 -> x0, starting transfers between devices: 6.33 us -> none  [on_device(): lax.all_to_all(block_norm, 'grp', split_axis=1, concat_axis=0, tiled=True)]
    all_to_all x1 -> x0, waiting for transfers between devices: 5.98 us -> none  [on_device(): lax.all_to_all(block_norm, 'grp', split_axis=1, concat_axis=0, tiled=True)]
  transfers between devices with their start and end apart: 3 -> 0, of which waited for: 2 -> 0; matrix products, arithmetic and copies ran while one was open for 1% -> 0% of each run, Pallas kernels for 0% -> 0%
where the time goes in v1:
time: 76 us; the launch traced here: 75.5 us
  Pallas kernels  65.5 us (86%)
  local copies, waits for them, and re-layouts  9.78 us (13%)
    pallas_call x1, Pallas kernels, on_device(): pl.pallas_call(functools.partial(kernel, S, G), out_shape=jax.ShapeDtypeS...  65.5 us
    unnamed x15, local copies, waits for them, and re-layouts  7.97 us

profile of v1, /device:TPU:0, one launch (start us, length us, event | category | flops | bytes accessed | tf_op | source)
XLA Modules:
  0.0 75.5 jit_solution(6416456367271011795)
XLA Ops:
  0.0 0.7 broadcast_in_dim.22
  0.7 0.1 broadcast_in_dim.23
  0.8 0.1 add.20
  0.9 0.1 fusion
  1.0 0.1 pad_maximum_fusion
  1.1 0.1 broadcast_in_dim.24.lens
  1.2 0.7 pad.4
  1.9 0.1 broadcast_in_dim.20
  2.0 0.1 broadcast_in_dim.21.acts
  2.0 0.0 copy-start
  2.0 1.2 %copy-done = bf16[512,1024]{1,0:T(8,128)(2,1)S(1)} copy-done((bf16[512,1024]{1,0:T(8,128)(2,1)S(1)}, bf16[512,1024]{1,0:T(8,128)(2,1)}, u32[]{:S(2)}) %copy-start) | copy-done | bytes 1048600
  3.3 0.0 copy-start.1
  3.3 1.2 %copy-done.1 = bf16[512,1024]{1,0:T(8,128)(2,1)S(1)} copy-done((bf16[512,1024]{1,0:T(8,128)(2,1)S(1)}, bf16[512,1024]{1,0:T(8,128)(2,1)}, u32[]{:S(2)}) %copy-start.1) | copy-done | bytes 1048600
  4.5 0.0 copy-start.2
  4.5 1.2 %copy-done.2 = bf16[512,1024]{1,0:T(8,128)(2,1)S(1)} copy-done((bf16[512,1024]{1,0:T(8,128)(2,1)S(1)}, bf16[512,1024]{1,0:T(8,128)(2,1)}, u32[]{:S(2)}) %copy-start.2) | copy-done | bytes 1048600
  5.7 0.0 copy-start.3
  5.7 1.2 %copy-done.3 = bf16[512,1024]{1,0:T(8,128)(2,1)S(1)} copy-done((bf16[512,1024]{1,0:T(8,128)(2,1)S(1)}, bf16[512,1024]{1,0:T(8,128)(2,1)}, u32[]{:S(2)}) %copy-start.3) | copy-done | bytes 1048600
  6.9 0.0 copy-start.4
  6.9 1.0 %copy-done.4 = bf16[64,4096]{1,0:T(8,128)(2,1)S(1)} copy-done((bf16[64,4096]{1,0:T(8,128)(2,1)S(1)}, bf16[64,4096]{1,0:T(8,128)(2,1)}, u32[]{:S(2)}) %copy-start.4) | copy-done | bytes 524312
  8.0 0.0 copy-start.5
  8.0 0.7 copy-done.5
  8.7 0.0 copy-start.6
  8.7 0.7 copy-done.6
  9.4 65.5 %shard_map.118 = f32[16,64]{1,0:T(8,128)S(1)} custom-call(s32[16,128]{1,0:T(8,128)S(1)} %broadcast_in_dim.21.acts, s32[16,128]{1,0:T(8,128)S(1)} %broadcast_in_dim.24.lens, f32[16,128]{1,0:T(8,128)S(1)} %get-tuple-element.8.cos_ref, f32[16,128]{1,0:T(8,128)S(1)} %get-tuple-element.9.sin_ref, f32[1,4096]{1,0:T(1,128)S(1)} %bitcast.5, f32[1,4096]{1,0:T(1,128)S(1)} %bitcast.6, ...), custom_call_target="tpu_custom_call" | custom-call | tf_op jit(solution)/shard_map/pallas_call | solution.py:427
  74.9 0.6 copy.14
  (3 shorter events, 0.0 us)
Async XLA Ops:
  2.0 1.2 %copy-start = (bf16[512,1024]{1,0:T(8,128)(2,1)S(1)}, bf16[512,1024]{1,0:T(8,128)(2,1)}, u32[]{:S(2)}) copy-start(bf16[512,1024]{1,0:T(8,128)(2,1)} %wq_h.1) | copy-start | bytes 3145732
  3.3 1.2 %copy-start.1 = (bf16[512,1024]{1,0:T(8,128)(2,1)S(1)}, bf16[512,1024]{1,0:T(8,128)(2,1)}, u32[]{:S(2)}) copy-start(bf16[512,1024]{1,0:T(8,128)(2,1)} %wk_h.1) | copy-start | bytes 3145732
  4.5 1.2 %copy-start.2 = (bf16[512,1024]{1,0:T(8,128)(2,1)S(1)}, bf16[512,1024]{1,0:T(8,128)(2,1)}, u32[]{:S(2)}) copy-start(bf16[512,1024]{1,0:T(8,128)(2,1)} %wv_h.1) | copy-start | bytes 3145732
  5.7 1.2 %copy-start.3 = (bf16[512,1024]{1,0:T(8,128)(2,1)S(1)}, bf16[512,1024]{1,0:T(8,128)(2,1)}, u32[]{:S(2)}) copy-start(bf16[512,1024]{1,0:T(8,128)(2,1)} %wo_h.1) | copy-start | bytes 3145732
  6.9 1.0 %copy-start.4 = (bf16[64,4096]{1,0:T(8,128)(2,1)S(1)}, bf16[64,4096]{1,0:T(8,128)(2,1)}, u32[]{:S(2)}) copy-start(bf16[64,4096]{1,0:T(8,128)(2,1)} %head_h.1) | copy-start | bytes 1572868
  8.0 0.7 copy-start.5
  8.7 0.7 copy-start.6

commit v2 on v1

--- a/solution.py
+++ b/solution.py
@@ -105,8 +105,9 @@
         ]
     ):
         copy = pltpu.make_async_copy(src, dst, load_sem.at[i])
+        loads.append(copy)
+    for copy in loads[:2]:
         copy.start()
-        loads.append(copy)
 
     barrier = pltpu.get_barrier_semaphore()
     total_devices = S * G
@@ -123,6 +124,13 @@
         return carry
 
     lax.fori_loop(1, total_devices, greet, 0)
+    loads[0].wait()
+    for copy in loads[2:]:
+        copy.start()
+    squares = jnp.zeros((bins, 128), jnp.float32)
+    for c in range(width // 128):
+        x = embed[:, c * 128 : (c + 1) * 128].astype(jnp.float32)
+        squares = squares + x * x
     pl.semaphore_wait(barrier, total_devices - 1)
 
     pending = []
@@ -147,11 +155,6 @@
     acts_all[g] = acts[...]
     ca = push("grp", G, g, lambda p: acts, acts_all.at[g], a_send, a_recv)
 
-    loads[0].wait()
-    squares = jnp.zeros((bins, 128), jnp.float32)
-    for c in range(width // 128):
-        x = embed[:, c * 128 : (c + 1) * 128].astype(jnp.float32)
-        squares = squares + x * x
     inv = lax.rsqrt(jnp.sum(squares, axis=-1, keepdims=True) * (1.0 / width) + 1e-05)
     block = pl.ds(pl.multiple_of(g * RB, RB), RB)
     table = (embed[:, block].astype(jnp.float32) * inv * gain_ref[:, block]).astype(jnp.bfloat16)
@@ -161,15 +164,18 @@
     picked = acts_all[...].reshape(G * RW, 128)[:, :1]
     onehot = jnp.where(lane_bin == picked, 1.0, 0.0).astype(jnp.bfloat16)
     rows = dot(onehot, table).astype(jnp.bfloat16)
+
+    def push_part(i):
+        return push(
+            "grp", G, g, lambda p: part.at[i, p], got.at[i, g], b_send.at[i], b_recv.at[i]
+        )
+
     cb = []
     for i in range(3):
         loads[1 + i].wait()
         part[i] = dot(rows, w3[i]).astype(jnp.bfloat16).reshape(G, RW, CB)
-        cb.append(
-            push(
-                "grp", G, g, lambda p, i=i: part.at[i, p], got.at[i, g], b_send.at[i], b_recv.at[i]
-            )
-        )
+        if i == 0:
+            cb.append(push_part(0))
     cols = pl.ds(pl.multiple_of(s * CB, CB), CB)
     own_hot = jnp.where(
         lax.broadcasted_iota(jnp.int32, (RW, bins), 1) == acts[:, :1], 1.0, 0.0
@@ -179,6 +185,9 @@
     def summed(i):
         for c in cb[i]:
             c.wait_recv()
+        if i == 0:
+            cb.append(push_part(1))
+            cb.append(push_part(2))
         total = part[i, g].astype(jnp.float32)
         for k in range(1, G):
             total = total + got[i, lax.rem(g + (G - k), G)].astype(jnp.float32)
@@ -202,21 +211,35 @@
 
     def attend(owner):
         q = qall[owner].astype(jnp.float32)
+        heads = [
+            pl.ds(pl.multiple_of(owner * CB + j * HEAD_DIM, HEAD_DIM), HEAD_DIM) for j in range(LH)
+        ]
+        raw = [
+            [
+                dot_t(
+                    q[r * PAD : (r + 1) * PAD, j * HEAD_DIM : (j + 1) * HEAD_DIM].astype(
+                        jnp.bfloat16
+                    ),
+                    kc[r, :, heads[j]],
+                )
+                for j in range(LH)
+            ]
+            for r in range(robots)
+        ]
         for r in range(robots):
             low = r * PAD
+            score = jnp.where(valid[r], jnp.stack(raw[r]) * scale, NEG)
+            top = jnp.max(score, axis=-1, keepdims=True)
+            e = jnp.where(valid[r], jnp.exp(score - top), 0.0)
+            total = jnp.sum(e, axis=-1, keepdims=True)
             tops = jnp.zeros((PAD, 128), jnp.float32)
             totals = jnp.zeros((PAD, 128), jnp.float32)
             for j in range(LH):
-                lanes = pl.ds(pl.multiple_of(owner * CB + j * HEAD_DIM, HEAD_DIM), HEAD_DIM)
-                qh = q[low : low + PAD, j * HEAD_DIM : (j + 1) * HEAD_DIM].astype(jnp.bfloat16)
-                score = jnp.where(valid[r], dot_t(qh, kc[r, :, lanes]) * scale, NEG)
-                top = jnp.max(score, axis=-1, keepdims=True)
-                e = jnp.where(valid[r], jnp.exp(score - top), 0.0)
-                tops = jnp.where(lane == j, top, tops)
-                totals = jnp.where(lane == j, jnp.sum(e, axis=-1, keepdims=True), totals)
                 acc_out[owner, low : low + PAD, j * HEAD_DIM : (j + 1) * HEAD_DIM] = dot(
-                    e.astype(jnp.bfloat16), vc[r, :, lanes]
+                    e[j].astype(jnp.bfloat16), vc[r, :, heads[j]]
                 )
+                tops = jnp.where(lane == j, top[j], tops)
+                totals = jnp.where(lane == j, total[j], totals)
             st_out[owner, 0, low : low + PAD, :] = tops
             st_out[owner, 1, low : low + PAD, :] = totals
 
@@ -419,7 +442,7 @@
     cos2 = jnp.concatenate([cosine, cosine], axis=1)
     sin2 = jnp.concatenate([-sine, sine], axis=1)
     vmem = pl.BlockSpec(memory_space=pltpu.VMEM)
-    hbm = pl.BlockSpec(memory_space=pl.ANY)
+    hbm = pl.BlockSpec(memory_space=pltpu.HBM)
     bf, f32 = jnp.bfloat16, jnp.float32
     bins_dev = head.shape[0]
     V = pltpu.VMEM
@@ -471,7 +494,7 @@
             D((S,)),
         ],
         compiler_params=pltpu.CompilerParams(
-            collective_id=0, has_side_effects=True, vmem_limit_bytes=48 * 2**20
+            collective_id=0, has_side_effects=True, vmem_limit_bytes=56 * 2**20
         ),
     )(
         acts,

time: 76 us -> 63.2 us (0.83)
  Pallas kernels: 65.5 us -> 57.7 us
  local copies, waits for them, and re-layouts: 9.78 us -> 4.29 us
    pallas_call x1, Pallas kernels: 65.5 us -> 57.7 us  [on_device(): pl.pallas_call(functools.partial(kernel, S, G), out_shape=jax.ShapeDtypeS...]
    unnamed x15 -> x1, local copies, waits for them, and re-layouts: 7.97 us -> 1.29 us
where the time goes in v2:
time: 63.2 us; the launch traced here: 62.8 us
  Pallas kernels  57.7 us (91%)
  local copies, waits for them, and re-layouts  4.29 us (7%)
  other arithmetic  0.82 us (1%)
    pallas_call x1, Pallas kernels, on_device(): pl.pallas_call(functools.partial(kernel, S, G), out_shape=jax.ShapeDtypeS...  57.7 us
    broadcast_in_dim x3, local copies, waits for them, and re-layouts, on_device(): lens = jnp.broadcast_to(jnp.repeat(lengths, PAD)[:, None], (RW, 128))  1.47 us
    unnamed x1, local copies, waits for them, and re-layouts  1.29 us

profile of v2, /device:TPU:0, one launch (start us, length us, event | category | flops | bytes accessed | tf_op | source)
XLA Modules:
  0.0 62.8 jit_solution(16715664011664812806)
XLA Ops:
  0.0 0.7 %broadcast_in_dim.22 = s32[2,8]{1,0:T(2,128)S(1)} broadcast(s32[2]{0:T(128)} %param.13), dimensions={0} | broadcast | bytes 72 | tf_op jit(solution)/shard_map/broadcast_in_dim | solution.py:435
  0.7 0.1 broadcast_in_dim.23
  0.8 0.1 add.20
  0.9 0.1 fusion
  1.0 0.7 %pad_maximum_fusion = (f32[16,128]{1,0:T(8,128)}, f32[16,128]{1,0:T(8,128)}) fusion(f32[16,64]{1,0:T(8,128)S(1)} %get-tuple-element.7, f32[16,64]{1,0:T(8,128)S(1)} %get-tuple-element.6, f32[16,64]{1,0:T(8,128)S(1)} %get-tuple-element.5), kind=kLoop, calls=%fused_computation.2 | loop fusion | flops 4096 | bytes 28672 | tf_op jit(solution)/shard_map/concatenate | solution.py:442
  1.7 0.7 %broadcast_in_dim.24.lens = s32[16,128]{1,0:T(8,128)} broadcast(s32[16]{0:T(128)S(1)} %broadcast_in_dim.23), dimensions={0} | broadcast | bytes 8256 | tf_op jit(solution)/shard_map/broadcast_in_dim | solution.py:435
  2.4 0.7 %pad.4 = s32[2,8]{1,0:T(2,128)S(1)} pad(s32[2,7]{1,0:T(2,128)} %param.12, s32[]{:T(128)} %constant.3.clone.1), padding=0_0x0_1 | pad | bytes 124 | tf_op jit(solution)/shard_map/jit(_pad)/pad | solution.py:433
  3.1 0.1 broadcast_in_dim.20
  3.2 0.7 %broadcast_in_dim.21.acts = s32[16,128]{1,0:T(8,128)} broadcast(s32[16]{0:T(128)S(1)} %broadcast_in_dim.20), dimensions={0} | broadcast | bytes 8256 | tf_op jit(solution)/shard_map/broadcast_in_dim | solution.py:434
  3.8 57.7 %shard_map.118 = f32[16,64]{1,0:T(8,128)} custom-call(s32[16,128]{1,0:T(8,128)} %broadcast_in_dim.21.acts, s32[16,128]{1,0:T(8,128)} %broadcast_in_dim.24.lens, f32[16,128]{1,0:T(8,128)} %get-tuple-element.8.cos_ref, f32[16,128]{1,0:T(8,128)} %get-tuple-element.9.sin_ref, f32[1,4096]{1,0:T(1,128)} %bitcast.5, f32[1,4096]{1,0:T(1,128)} %bitcast.6, ...), custom_call_target="tpu_custom_call" | custom-call | tf_op jit(solution)/shard_map/pallas_call | solution.py:450
  61.5 1.3 %copy.14 = f32[2,7,64]{2,0,1:T(2,128)} copy(f32[2,7,64]{2,1,0:T(8,128)} %bitcast.4) | data formatting | bytes 7168
  (3 shorter events, 0.0 us)
